TPU v7x, 512 devices: a whole 4x4x16 slice. The times are simulated.
512 devices in a mesh: seq: 8 (over y, core), dp: 64 (over z, x).
Axes of the slice: x: 4, y: 4, z: 16, core: 2. Of those that a mesh axis runs over, the one named last changes fastest.
Arguments:
- frames: bfloat16 [128, 512, 1024], P('dp', 'seq'), may hold values from -6 to 6
- lengths: int32 [128], P('dp'), may hold values from 128 to 512, as said below
- w_qkv: bfloat16 [1024, 3072], P('dp'), may hold values from -4 to 4
- w_out: bfloat16 [1024, 1024], P('dp'), may hold values from -0.1875 to 0.1875
- w_point: bfloat16 [1024, 1024], P('dp'), may hold values from -0.1875 to 0.1875
- w_depth: float32 [9, 1024], replicated, may hold values from -2 to 2
Outputs:
- layer_out: bfloat16 [128, 512, 1024], P('dp', 'seq')
Inputs may be any that keep to these rules, and one draw needn't show every extreme that they name: `lengths`: every recording has at least 128 valid frames; some recording fills all 512.
All inputs are finite; a program needn't handle non-finite values.
Results may differ from a plain program's by a relative error of at most 0.014.
Values may be sent and summed in bfloat16 or wider, within the bound.
A program may use at most 64 MiB of HBM per device.

v0:
```python
import jax
import jax.numpy as jnp
from jax import lax
from jax.sharding import PartitionSpec as P

D = 1024
HEADS = 8
KERNEL = 9
HDIM = 128


def with_halo(cells, sides, width):
    for axis, dim in sides:
        count = lax.axis_size(axis)
        ends = count - 1
        head = lax.slice_in_dim(cells, 0, width, axis=dim)
        tail = lax.slice_in_dim(cells, cells.shape[dim] - width, cells.shape[dim], axis=dim)
        cells = jnp.concatenate(
            [
                lax.ppermute(tail, axis, [(i, (i + 1) % count) for i in range(ends)]),
                cells,
                lax.ppermute(head, axis, [((i + 1) % count, i) for i in range(ends)]),
            ],
            axis=dim,
        )
    return cells


def norm_rows(values):
    centre = jnp.mean(values, axis=-1, keepdims=True)
    spread = jnp.mean(jnp.square(values - centre), axis=-1, keepdims=True)
    return (values - centre) * lax.rsqrt(spread + 1e-05)


def attend(packed, length):
    total_rows = packed.shape[0]
    queries = packed[:, 0]
    keys_all = packed[:, 1]
    values_all = packed[:, 2]
    scaling = packed.shape[-1] ** (-0.5)
    block = min(512, total_rows)
    keep_mask = jnp.arange(total_rows) < length
    query_blocks = queries.reshape(total_rows // block, block, queries.shape[1], queries.shape[2])

    def one_block(qblock):
        scores = (
            jnp.einsum("qnd,knd->nqk", qblock, keys_all, preferred_element_type=jnp.float32)
            * scaling
        )
        scores = jnp.where(keep_mask[None, None, :], scores, -1e30)
        highest = jnp.max(scores, axis=-1, keepdims=True)
        powers = jnp.exp(scores - highest)
        totals = jnp.sum(powers, axis=-1, keepdims=True)
        probs = (powers / totals).astype(jnp.bfloat16)
        mixed = jnp.einsum("nqk,knd->qnd", probs, values_all, preferred_element_type=jnp.float32)
        return mixed.astype(jnp.bfloat16)

    return lax.map(one_block, query_blocks).reshape(total_rows, queries.shape[1], queries.shape[2])


def attend_many(packed, lengths):

    def one_recording(pair):
        return attend(pair[0], pair[1])

    return lax.map(one_recording, (packed, lengths))


def add_rows(left, piece):
    return jnp.dot(left, piece, preferred_element_type=jnp.float32)


def body(frames, lengths, w_qkv, w_out, w_point, w_depth):
    count = frames.shape[0]
    rows_here = frames.shape[1]
    seq_size = lax.axis_size("seq")
    per_device = HEADS // seq_size
    flat_rows = count * rows_here
    local = frames.reshape(flat_rows, D)
    normed = norm_rows(local.astype(jnp.float32)).astype(jnp.bfloat16)
    qkv = add_rows(normed, lax.all_gather(w_qkv, "dp", axis=0, tiled=True))
    qkv = qkv.astype(jnp.bfloat16).reshape(count, rows_here, 3, seq_size, per_device, HDIM)
    received = lax.all_to_all(qkv, "seq", split_axis=3, concat_axis=1, tiled=True)
    some = received.shape[4]
    packed = received.reshape(count, received.shape[1], 3, some, HDIM)
    mixed = attend_many(packed, lengths)
    heads_out = mixed.reshape(count, received.shape[1], 1, some, HDIM)
    attended = lax.all_to_all(heads_out, "seq", split_axis=1, concat_axis=2, tiled=True).reshape(
        flat_rows, D
    )
    projected = add_rows(attended, lax.all_gather(w_out, "dp", axis=0, tiled=True))
    resid = (local.astype(jnp.float32) + projected).astype(jnp.bfloat16)
    position = lax.axis_index("seq") * rows_here + jnp.arange(rows_here)
    valid = (position[None, :] < lengths[:, None]).reshape(flat_rows, 1)
    conv_in = jnp.where(valid, norm_rows(resid.astype(jnp.float32)), 0.0).astype(jnp.bfloat16)
    conv_in = conv_in.reshape(count, rows_here, D)
    padded = with_halo(conv_in, (("seq", 1),), KERNEL // 2).astype(jnp.float32)
    depth = jnp.zeros((count, rows_here, D), jnp.float32)
    for offset in range(KERNEL):
        depth = depth + padded[:, offset : offset + rows_here] * w_depth[offset]
    gated = (depth * jax.nn.sigmoid(depth)).astype(jnp.bfloat16).reshape(flat_rows, D)
    pointed = add_rows(gated, lax.all_gather(w_point, "dp", axis=0, tiled=True))
    result = jnp.where(valid, resid.astype(jnp.float32) + pointed, 0.0).astype(jnp.bfloat16)
    return result.reshape(count, rows_here, D)


def solution(mesh):
    in_specs = (P("dp", "seq", None), P("dp"), P("dp", None), P("dp", None), P("dp", None), P())
    out_specs = P("dp", "seq", None)
    return jax.shard_map(body, mesh=mesh, in_specs=in_specs, out_specs=out_specs, check_vma=False)
```

profile of v0, /device:TPU:8, one launch (start us, length us, event | category | flops | bytes accessed | tf_op | source)
XLA Modules:
  0.0 454.9 jit_solution(9650559894608089350)
XLA Ops:
  6.5 0.7 all-gather.4.cloned.1.call-update
  7.3 0.7 all-gather.6.cloned.1.call-update
  8.0 1.1 convert_reduce_fusion
  9.2 1.2 multiply_reduce_fusion.1
  10.4 1.2 fusion.18
  11.6 154.8 %all-gather.4.cloned.1.call-done = bf16[1024,3072]{1,0:T(8,128)(2,1)} async-done(((bf16[16,3072]{1,0:T(8,128)(2,1)}), bf16[1024,3072]{1,0:T(8,128)(2,1)}) %all-gather.4.cloned.1.call-update) | async-done | bytes 6291472 | tf_op jit(solution)/shard_map/all_gather | solution.py:81
  166.4 3.8 fusion.4
  170.4 1.1 copy.12
  171.4 4.8 %all-to-all-start = ((bf16[2,64,3,8,1,128]{5,1,2,0,4,3:T(8,128)(2,1)}), bf16[2,64,3,8,1,128]{5,1,2,0,4,3:T(8,128)(2,1)S(1)}, u32[]{:S(2)}, u32[]{:S(2)}) async-start(bf16[2,64,3,8,1,128]{5,1,2,0,4,3:T(8,128)(2,1)} %copy.12), calls=%async_computation | async-start | bytes 1572864 | tf_op jit(solution)/shard_map/all_to_all | solution.py:83
  176.3 0.7 all-gather.8.cloned.1.call-update
  177.0 11.0 %all-to-all-done = bf16[2,64,3,8,1,128]{5,1,2,0,4,3:T(8,128)(2,1)S(1)} async-done(((bf16[2,64,3,8,1,128]{5,1,2,0,4,3:T(8,128)(2,1)}), bf16[2,64,3,8,1,128]{5,1,2,0,4,3:T(8,128)(2,1)S(1)}, u32[]{:S(2)}, u32[]{:S(2)}) %all-to-all-start) | async-done | bytes 786464 | tf_op jit(solution)/shard_map/all_to_all | solution.py:83
  188.0 4.2 while.10
  188.1 0.6 dynamic_slice.15
  192.2 0.9 copy.15
  193.1 4.8 %all-to-all-start.1 = ((bf16[2,512,1,1,128]{4,0,3,2,1:T(2,128)(2,1)}), bf16[2,512,1,1,128]{4,0,3,2,1:T(2,128)(2,1)S(1)}, u32[]{:S(2)}, u32[]{:S(2)}) async-start(bf16[2,512,1,1,128]{4,0,3,2,1:T(2,128)(2,1)} %bitcast.13), calls=%async_computation.1 | async-start | bytes 524288 | tf_op jit(solution)/shard_map/all_to_all | solution.py:88
  198.0 5.9 %all-to-all-done.1 = bf16[2,512,1,1,128]{4,0,3,2,1:T(2,128)(2,1)S(1)} async-done(((bf16[2,512,1,1,128]{4,0,3,2,1:T(2,128)(2,1)}), bf16[2,512,1,1,128]{4,0,3,2,1:T(2,128)(2,1)S(1)}, u32[]{:S(2)}, u32[]{:S(2)}) %all-to-all-start.1) | async-done | bytes 262176 | tf_op jit(solution)/shard_map/all_to_all | solution.py:88
  204.2 101.5 %all-gather.6.cloned.1.call-done = bf16[1024,1024]{1,0:T(8,128)(2,1)} async-done(((bf16[16,1024]{1,0:T(8,128)(2,1)}), bf16[1024,1024]{1,0:T(8,128)(2,1)}) %all-gather.6.cloned.1.call-update) | async-done | bytes 2097168 | tf_op jit(solution)/shard_map/all_gather | solution.py:91
  305.7 2.1 fusion.24
  308.2 1.9 collective-permute-start
  310.2 3.6 collective-permute-start.1
  313.9 1.4 collective-permute-done.1
  315.3 0.6 multiply_convert_fusion
  316.0 129.6 %all-gather.8.cloned.1.call-done = bf16[1024,1024]{1,0:T(8,128)(2,1)} async-done(((bf16[16,1024]{1,0:T(8,128)(2,1)}), bf16[1024,1024]{1,0:T(8,128)(2,1)}) %all-gather.8.cloned.1.call-update) | async-done | bytes 2097168 | tf_op jit(solution)/shard_map/all_gather | solution.py:102
  445.6 2.7 fusion.6
  (40 shorter events, 4.8 us)
Async XLA Ops:
  6.5 159.8 %all-gather.4.cloned.1.call-start = ((), (), s32[]{:S(2)}) async-start(), calls=%async_computation.2 | async-start | bytes 6389760 | tf_op jit(solution)/shard_map/all_gather | solution.py:81
  7.3 298.4 %all-gather.6.cloned.1.call-start = ((), (), s32[]{:S(2)}) async-start(), calls=%async_computation.3 | async-start | bytes 2129920 | tf_op jit(solution)/shard_map/all_gather | solution.py:91
  170.3 17.7 %copy-start.2 = (s32[2]{0:T(128)S(1)}, s32[2]{0:T(128)}, u32[]{:S(2)}) copy-start(s32[2]{0:T(128)} %param.9) | copy-start | bytes 28
  171.4 16.5 %all-to-all-start = ((bf16[2,64,3,8,1,128]{5,1,2,0,4,3:T(8,128)(2,1)}), bf16[2,64,3,8,1,128]{5,1,2,0,4,3:T(8,128)(2,1)S(1)}, u32[]{:S(2)}, u32[]{:S(2)}) async-start(bf16[2,64,3,8,1,128]{5,1,2,0,4,3:T(8,128)(2,1)} %copy.12), calls=%async_computation | async-start | bytes 1572864 | tf_op jit(solution)/shard_map/all_to_all | solution.py:83
  176.3 269.3 %all-gather.8.cloned.1.call-start = ((), (), s32[]{:S(2)}) async-start(), calls=%async_computation.4 | async-start | bytes 2129920 | tf_op jit(solution)/shard_map/all_gather | solution.py:102
  192.2 113.5 %copy-start = (bf16[2,64,1024]{2,1,0:T(8,128)(2,1)S(1)}, bf16[2,64,1024]{2,1,0:T(8,128)(2,1)}, u32[]{:S(2)}) copy-start(bf16[2,64,1024]{2,1,0:T(8,128)(2,1)} %param.8) | copy-start | bytes 786436
  193.1 10.9 %all-to-all-start.1 = ((bf16[2,512,1,1,128]{4,0,3,2,1:T(2,128)(2,1)}), bf16[2,512,1,1,128]{4,0,3,2,1:T(2,128)(2,1)S(1)}, u32[]{:S(2)}, u32[]{:S(2)}) async-start(bf16[2,512,1,1,128]{4,0,3,2,1:T(2,128)(2,1)} %bitcast.13), calls=%async_computation.1 | async-start | bytes 524288 | tf_op jit(solution)/shard_map/all_to_all | solution.py:88
  305.7 8.2 %copy-start.1 = (f32[9,1024]{1,0:T(8,128)S(1)}, f32[9,1024]{1,0:T(8,128)}, u32[]{:S(2)}) copy-start(f32[9,1024]{1,0:T(8,128)} %param.13) | copy-start | bytes 110596
  308.2 5.6 %collective-permute-start = (bf16[2,4,1024]{2,1,0:T(4,128)(2,1)S(1)}, bf16[2,4,1024]{2,1,0:T(4,128)(2,1)S(1)}, u32[]{:S(2)}, u32[]{:S(2)}) collective-permute-start(bf16[2,4,1024]{2,1,0:T(4,128)(2,1)S(1)} %get-tuple-element.64), channel_id=1, source_target_pairs={{0,64},{64,128},{128,192},{192,256},{256,320},{320,384},{384,448},... | collective-permute-start | bytes 49160 | tf_op jit(solution)/shard_map/ppermute | solution.py:20
  310.2 5.1 %collective-permute-start.1 = (bf16[2,4,1024]{2,1,0:T(4,128)(2,1)S(1)}, bf16[2,4,1024]{2,1,0:T(4,128)(2,1)S(1)}, u32[]{:S(2)}, u32[]{:S(2)}) collective-permute-start(bf16[2,4,1024]{2,1,0:T(4,128)(2,1)S(1)} %get-tuple-element.65), channel_id=1, source_target_pairs={{64,0},{128,64},{192,128},{256,192},{320,256},{384,320},{448,384},... | collective-permute-start | bytes 49160 | tf_op jit(solution)/shard_map/ppermute | solution.py:22
Sparse Core Ops, SparseCore 0:
  10.3 156.0 all-gather.3
  169.3 136.2 all-gather.5
  308.6 136.9 all-gather.7
where the time goes:
time: 455 us
  waiting for transfers between devices  406 us (89%)
  starting transfers between devices  15.2 us (3%)
  between operations  13.3 us (3%)
  matrix products  10 us (2%)
  other arithmetic  6.13 us (1%)
    all_gather x1, waiting for transfers between devices, body(): qkv = add_rows(normed, lax.all_gather(w_qkv, 'dp', axis=0, tiled=True))  155 us
    all_gather x1, waiting for transfers between devices, body(): pointed = add_rows(gated, lax.all_gather(w_point, 'dp', axis=0, tiled=True))  130 us
    all_gather x1, waiting for transfers between devices, body(): lax.all_gather(w_out, 'dp', axis=0, tiled=True)  101 us
    all_to_all x1, waiting for transfers between devices, body(): lax.all_to_all(qkv, 'seq', split_axis=3, concat_axis=1, tiled=True)  11 us
  transfers between devices with their start and end apart: 7, of which 6 were waited for; matrix products, arithmetic and copies ran while one was open for 4% of the time, Pallas kernels for 0%

commit v1 on v0

--- a/solution.py
+++ b/solution.py
@@ -78,7 +78,12 @@
     flat_rows = count * rows_here
     local = frames.reshape(flat_rows, D)
     normed = norm_rows(local.astype(jnp.float32)).astype(jnp.bfloat16)
-    qkv = add_rows(normed, lax.all_gather(w_qkv, "dp", axis=0, tiled=True))
+    qkv = add_rows(
+        normed,
+        jnp.concatenate(
+            lax.all_to_all(jnp.stack([w_qkv] * lax.axis_size("dp")), "dp", 0, 0), axis=0
+        ),
+    )
     qkv = qkv.astype(jnp.bfloat16).reshape(count, rows_here, 3, seq_size, per_device, HDIM)
     received = lax.all_to_all(qkv, "seq", split_axis=3, concat_axis=1, tiled=True)
     some = received.shape[4]

time: 455 us -> 479 us (1.053)
  starting transfers between devices: 15.2 us -> 34.2 us
    all_to_all x0 -> x1, waiting for transfers between devices: none -> 292 us  [body(): lax.all_to_all(jnp.stack([w_qkv] * lax.axis_size('dp')), 'dp', 0, 0)]
    all_gather x1 -> x0, waiting for transfers between devices: 155 us -> none  [body(): qkv = add_rows(normed, lax.all_gather(w_qkv, 'dp', axis=0, tiled=True))]
    all_gather x1, waiting for transfers between devices: 101 us -> 0.02 us  [body(): lax.all_gather(w_out, 'dp', axis=0, tiled=True)]
    all_gather x1, waiting for transfers between devices: 130 us -> 97.8 us  [body(): pointed = add_rows(gated, lax.all_gather(w_point, 'dp', axis=0, tiled=True))]
    all_to_all x0 -> x1, starting transfers between devices: none -> 18.9 us  [body(): lax.all_to_all(jnp.stack([w_qkv] * lax.axis_size('dp')), 'dp', 0, 0)]
  transfers between devices with their start and end apart: 7 -> 7, of which waited for: 6 -> 5; matrix products, arithmetic and copies ran while one was open for 4% -> 3% of each run, Pallas kernels for 0% -> 0%
where the time goes in v1:
time: 479 us
  waiting for transfers between devices  409 us (85%)
  starting transfers between devices  34.2 us (7%)
  between operations  13.6 us (3%)
  matrix products  10 us (2%)
  local copies, waits for them, and re-layouts  8.13 us (2%)
    all_to_all x1, waiting for transfers between devices, body(): lax.all_to_all(jnp.stack([w_qkv] * lax.axis_size('dp')), 'dp', 0, 0)  292 us
    all_gather x1, waiting for transfers between devices, body(): pointed = add_rows(gated, lax.all_gather(w_point, 'dp', axis=0, tiled=True))  97.8 us
    all_to_all x1, starting transfers between devices, body(): lax.all_to_all(jnp.stack([w_qkv] * lax.axis_size('dp')), 'dp', 0, 0)  18.9 us
    all_to_all x1, waiting for transfers between devices, body(): lax.all_to_all(qkv, 'seq', split_axis=3, concat_axis=1, tiled=True)  10.9 us
  transfers between devices with their start and end apart: 7, of which 5 were waited for; matrix products, arithmetic and copies ran while one was open for 3% of the time, Pallas kernels for 0%

profile of v1, /device:TPU:8, one launch (start us, length us, event | category | flops | bytes accessed | tf_op | source)
XLA Modules:
  0.0 478.7 jit_solution(18178556953295126168)
XLA Ops:
  6.5 4.3 stack.2
  10.9 18.9 %all-to-all-start = ((bf16[64,16,3072]{2,1,0:T(8,128)(2,1)}), bf16[64,16,3072]{2,1,0:T(8,128)(2,1)}, u32[]{:S(2)}, u32[]{:S(2)}) async-start(bf16[64,16,3072]{2,1,0:T(8,128)(2,1)} %stack.2), calls=%async_computation | async-start | bytes 12582912 | tf_op jit(solution)/shard_map/all_to_all | solution.py:84
  29.8 0.7 all-gather.3.cloned.1.call-update
  31.1 291.7 %all-to-all-done = bf16[64,16,3072]{2,1,0:T(8,128)(2,1)} async-done(((bf16[64,16,3072]{2,1,0:T(8,128)(2,1)}), bf16[64,16,3072]{2,1,0:T(8,128)(2,1)}, u32[]{:S(2)}, u32[]{:S(2)}) %all-to-all-start) | async-done | bytes 6291488 | tf_op jit(solution)/shard_map/all_to_all | solution.py:84
  322.9 3.8 fusion.4
  326.8 1.1 copy.12
  327.9 4.9 %all-to-all-start.1 = ((bf16[2,64,3,8,1,128]{5,1,2,0,4,3:T(8,128)(2,1)}), bf16[2,64,3,8,1,128]{5,1,2,0,4,3:T(8,128)(2,1)S(1)}, u32[]{:S(2)}, u32[]{:S(2)}) async-start(bf16[2,64,3,8,1,128]{5,1,2,0,4,3:T(8,128)(2,1)} %copy.12), calls=%async_computation.1 | async-start | bytes 1572864 | tf_op jit(solution)/shard_map/all_to_all | solution.py:88
  332.9 0.7 all-gather.5.cloned.1.call-update
  333.6 10.9 %all-to-all-done.1 = bf16[2,64,3,8,1,128]{5,1,2,0,4,3:T(8,128)(2,1)S(1)} async-done(((bf16[2,64,3,8,1,128]{5,1,2,0,4,3:T(8,128)(2,1)}), bf16[2,64,3,8,1,128]{5,1,2,0,4,3:T(8,128)(2,1)S(1)}, u32[]{:S(2)}, u32[]{:S(2)}) %all-to-all-start.1) | async-done | bytes 786464 | tf_op jit(solution)/shard_map/all_to_all | solution.py:88
  344.6 4.3 while.10
  344.7 0.6 dynamic_slice.15
  345.3 0.6 iota_compare_fusion.2
  346.8 0.6 dynamic_slice.15
  347.4 0.6 iota_compare_fusion.2
  348.9 0.9 copy.15
  349.8 4.8 all-to-all-start.2
  354.8 5.9 %all-to-all-done.2 = bf16[2,512,1,1,128]{4,0,3,2,1:T(2,128)(2,1)S(1)} async-done(((bf16[2,512,1,1,128]{4,0,3,2,1:T(2,128)(2,1)}), bf16[2,512,1,1,128]{4,0,3,2,1:T(2,128)(2,1)S(1)}, u32[]{:S(2)}, u32[]{:S(2)}) %all-to-all-start.2) | async-done | bytes 262176 | tf_op jit(solution)/shard_map/all_to_all | solution.py:93
  361.0 2.2 fusion.22
  363.5 1.9 collective-permute-start
  365.5 3.6 collective-permute-start.1
  369.2 1.4 collective-permute-done.1
  370.6 0.6 multiply_convert_fusion
  371.3 97.8 %all-gather.5.cloned.1.call-done = bf16[1024,1024]{1,0:T(8,128)(2,1)} async-done(((bf16[16,1024]{1,0:T(8,128)(2,1)}), bf16[1024,1024]{1,0:T(8,128)(2,1)}) %all-gather.5.cloned.1.call-update) | async-done | bytes 2097168 | tf_op jit(solution)/shard_map/all_gather | solution.py:107
  469.1 2.7 fusion.6
  (38 shorter events, 3.5 us)
Async XLA Ops:
  10.9 19.7 %copy-start = (bf16[2,64,1024]{2,1,0:T(8,128)(2,1)S(1)}, bf16[2,64,1024]{2,1,0:T(8,128)(2,1)}, u32[]{:S(2)}) copy-start(bf16[2,64,1024]{2,1,0:T(8,128)(2,1)} %param.8) | copy-start | bytes 786436
  10.9 312.0 %all-to-all-start = ((bf16[64,16,3072]{2,1,0:T(8,128)(2,1)}), bf16[64,16,3072]{2,1,0:T(8,128)(2,1)}, u32[]{:S(2)}, u32[]{:S(2)}) async-start(bf16[64,16,3072]{2,1,0:T(8,128)(2,1)} %stack.2), calls=%async_computation | async-start | bytes 12582912 | tf_op jit(solution)/shard_map/all_to_all | solution.py:84
  29.8 331.2 %all-gather.3.cloned.1.call-start = ((), (), s32[]{:S(2)}) async-start(), calls=%async_computation.3 | async-start | bytes 2129920 | tf_op jit(solution)/shard_map/all_gather | solution.py:96
  326.8 17.8 %copy-start.2 = (s32[2]{0:T(128)S(1)}, s32[2]{0:T(128)}, u32[]{:S(2)}) copy-start(s32[2]{0:T(128)} %param.9) | copy-start | bytes 28
  327.9 16.6 %all-to-all-start.1 = ((bf16[2,64,3,8,1,128]{5,1,2,0,4,3:T(8,128)(2,1)}), bf16[2,64,3,8,1,128]{5,1,2,0,4,3:T(8,128)(2,1)S(1)}, u32[]{:S(2)}, u32[]{:S(2)}) async-start(bf16[2,64,3,8,1,128]{5,1,2,0,4,3:T(8,128)(2,1)} %copy.12), calls=%async_computation.1 | async-start | bytes 1572864 | tf_op jit(solution)/shard_map/all_to_all | solution.py:88
  332.9 136.3 %all-gather.5.cloned.1.call-start = ((), (), s32[]{:S(2)}) async-start(), calls=%async_computation.4 | async-start | bytes 2129920 | tf_op jit(solution)/shard_map/all_gather | solution.py:107
  349.8 10.9 %all-to-all-start.2 = ((bf16[2,512,1,1,128]{4,0,3,2,1:T(2,128)(2,1)}), bf16[2,512,1,1,128]{4,0,3,2,1:T(2,128)(2,1)S(1)}, u32[]{:S(2)}, u32[]{:S(2)}) async-start(bf16[2,512,1,1,128]{4,0,3,2,1:T(2,128)(2,1)} %bitcast.15), calls=%async_computation.2 | async-start | bytes 524288 | tf_op jit(solution)/shard_map/all_to_all | solution.py:93
  361.0 8.2 %copy-start.1 = (f32[9,1024]{1,0:T(8,128)S(1)}, f32[9,1024]{1,0:T(8,128)}, u32[]{:S(2)}) copy-start(f32[9,1024]{1,0:T(8,128)} %param.13) | copy-start | bytes 110596
  363.5 5.6 %collective-permute-start = (bf16[2,4,1024]{2,1,0:T(4,128)(2,1)S(1)}, bf16[2,4,1024]{2,1,0:T(4,128)(2,1)S(1)}, u32[]{:S(2)}, u32[]{:S(2)}) collective-permute-start(bf16[2,4,1024]{2,1,0:T(4,128)(2,1)S(1)} %get-tuple-element.64), channel_id=1, source_target_pairs={{0,64},{64,128},{128,192},{192,256},{256,320},{320,384},{384,448},... | collective-permute-start | bytes 49160 | tf_op jit(solution)/shard_map/ppermute | solution.py:20
  365.5 5.1 %collective-permute-start.1 = (bf16[2,4,1024]{2,1,0:T(4,128)(2,1)S(1)}, bf16[2,4,1024]{2,1,0:T(4,128)(2,1)S(1)}, u32[]{:S(2)}, u32[]{:S(2)}) collective-permute-start(bf16[2,4,1024]{2,1,0:T(4,128)(2,1)S(1)} %get-tuple-element.65), channel_id=1, source_target_pairs={{64,0},{128,64},{192,128},{256,192},{320,256},{384,320},{448,384},... | collective-permute-start | bytes 49160 | tf_op jit(solution)/shard_map/ppermute | solution.py:22
Sparse Core Ops, SparseCore 0:
  33.6 195.9 all-gather.2
  336.6 132.4 all-gather.4
